TPU v7x, 32 devices: a whole 2x2x4 slice. The times are simulated.
32 devices in a mesh: frame: 8 (over z, y), audio: 4 (over x, core).
Axes of the slice: x: 2, y: 2, z: 4, core: 2. Of those that a mesh axis runs over, the one named last changes fastest.
Arguments:
- video: bfloat16 [25088, 768], P(('frame', 'audio')), may hold values from -6 to 6
- audio: bfloat16 [8192, 768], P(('frame', 'audio')), may hold values from -6 to 6
- w_query: bfloat16 [768, 768], replicated, may hold values from -9 to 9
- w_key: bfloat16 [768, 768], replicated, may hold values from -0.21875 to 0.21875
- w_value: bfloat16 [768, 768], replicated, may hold values from -0.21875 to 0.21875
- w_out: bfloat16 [768, 768], replicated, may hold values from -0.21875 to 0.21875
- grad_output: bfloat16 [25088, 768], P(('frame', 'audio')), may hold values from -6 to 6
- intersection_tiles: int32 [128, 8], P(('frame', 'audio')), may hold values from 0 to 63, as said below
- intersection_count: int32 [128], P(('frame', 'audio')), may hold values from 1 to 8
- tile_fill: int32 [64], P(('frame', 'audio')), may hold values from 32 to 128
Outputs:
- output: bfloat16 [25088, 768], P(('frame', 'audio'))
- grad_video: bfloat16 [25088, 768], P(('frame', 'audio'))
- grad_audio: bfloat16 [8192, 768], P(('frame', 'audio'))
- grad_w_query: float32 [768, 768], replicated
- grad_w_key: float32 [768, 768], replicated
- grad_w_value: float32 [768, 768], replicated
- grad_w_out: float32 [768, 768], replicated
Inputs may be any that keep to these rules, and one draw needn't show every extreme that they name: `intersection_tiles`: entries j < intersection_count[f] of frame f are distinct tiles of index in [(f // 4 - 2) * 2, (f // 4 + 3) * 2); other entries are any tile.
All inputs are finite; a program needn't handle non-finite values.
Results may differ from a plain program's by a relative error of at most 0.0085.
The roundings to bfloat16 on the way count: a program that leaves them out, or rounds other values in their place, can miss the bound.
Values may be sent and summed in bfloat16 or wider, within the bound.
A program may use at most 192 MiB of HBM per device.

v0:
```python
import functools
import math

import jax
import jax.numpy as jnp
from jax import lax
from jax.experimental import pallas as pl
from jax.experimental.pallas import tpu as pltpu
from jax.sharding import PartitionSpec as P

HEADS = 12
TILE = 128
REACH = 2
STREAMS = 3
MESH = pl.DeviceIdType.MESH
SIZES = (2, 4, 6, 8)


def neighbour(distance):
    inner, total = lax.axis_size("audio"), lax.axis_size("audio") * lax.axis_size("frame")
    index = lax.axis_index("frame") * inner + lax.axis_index("audio") + distance
    exists = (index >= 0) & (index < total)
    index = lax.rem(index + total, total)
    return (index // inner, lax.rem(index, inner)), exists


def other_offsets():
    return [offset for offset in range(-REACH, REACH + 1) if offset != 0]


def greet_neighbours(barrier, others=0):
    for offset in other_offsets():
        device, _ = neighbour(offset)
        pl.semaphore_signal(barrier, inc=1, device_id=device, device_id_type=MESH)
    pl.semaphore_wait(barrier, 2 * REACH + others)


def tile_rows(rows):
    return max(part for part in range(16, min(rows, 256) + 1, 16) if rows % part == 0)


def halo_kernel(
    rows_ref,
    fill_ref,
    normed_ref,
    grad_ref,
    w_query_ref,
    w_out_ref,
    window_ref,
    fills_ref,
    query_ref,
    dcontext_ref,
    send_sems,
    recv_sems,
):
    greet_neighbours(pltpu.get_barrier_semaphore())

    def copies(offset):
        device, exists = neighbour(offset)
        place = REACH - offset
        return exists, [
            pltpu.make_async_remote_copy(
                src_ref=source,
                dst_ref=target.at[place],
                send_sem=send_sems.at[i, place],
                recv_sem=recv_sems.at[i, place],
                device_id=device,
                device_id_type=MESH,
            )
            for i, (source, target) in enumerate(((rows_ref, window_ref), (fill_ref, fills_ref)))
        ]

    for offset in other_offsets():
        exists, pair = copies(offset)

        @pl.when(exists)
        def _():
            for copy in pair:
                copy.start()

    window_ref[REACH] = rows_ref[...]
    fills_ref[REACH] = fill_ref[...]
    for offset in other_offsets():
        _, exists = neighbour(-offset)
        place = REACH - offset

        @pl.when(jnp.logical_not(exists))
        def _():
            window_ref[place] = jnp.zeros(rows_ref.shape, rows_ref.dtype)
            fills_ref[place] = jnp.zeros(fill_ref.shape, fill_ref.dtype)

    part = tile_rows(normed_ref.shape[0])

    def project(i, carry):
        at = pl.ds(pl.multiple_of(i * part, 16), part)
        query_ref[at, :] = dot_nn(normed_ref[at, :], w_query_ref[...]).astype(query_ref.dtype)
        dcontext_ref[at, :] = dot_nt(grad_ref[at, :], w_out_ref[...]).astype(dcontext_ref.dtype)
        return carry

    lax.fori_loop(0, normed_ref.shape[0] // part, project, 0)
    for offset in other_offsets():
        exists, pair = copies(offset)
        _, comes = neighbour(-offset)

        @pl.when(exists)
        def _():
            for copy in pair:
                copy.wait_send()

        @pl.when(comes)
        def _():
            for copy in pair:
                copy.wait_recv()


def gather_halo(rows, fill, normed, grad, w_query, w_out):
    vmem = pl.BlockSpec(memory_space=pltpu.VMEM)
    spread = 2 * REACH + 1
    return pl.pallas_call(
        halo_kernel,
        in_specs=[vmem] * 6,
        out_specs=[vmem] * 4,
        out_shape=[
            jax.ShapeDtypeStruct((spread, *rows.shape), rows.dtype),
            jax.ShapeDtypeStruct((spread, *fill.shape), fill.dtype),
            jax.ShapeDtypeStruct(normed.shape, normed.dtype),
            jax.ShapeDtypeStruct(grad.shape, grad.dtype),
        ],
        scratch_shapes=[
            pltpu.SemaphoreType.DMA((2, spread)),
            pltpu.SemaphoreType.DMA((2, spread)),
        ],
        compiler_params=pltpu.CompilerParams(
            collective_id=1, has_side_effects=True, vmem_limit_bytes=32 * 1024 * 1024
        ),
        name="gather_halo",
    )(rows, fill, normed, grad, w_query, w_out)


def partner(axis, bit):
    me = lax.axis_index(axis)
    mine = lax.rem(me // (1 << bit), 2)
    other = me + (1 << bit) * (1 - 2 * mine)
    if axis == "frame":
        return (other, lax.axis_index("audio")), mine
    return (lax.axis_index("frame"), other), mine


def sum_kernel(
    bits,
    sums_refs,
    back_ref,
    context_ref,
    dquery_ref,
    video_ref,
    grad_ref,
    w_out_ref,
    w_query_ref,
    total_ref,
    returned_ref,
    output_ref,
    grad_video_ref,
    whole_recv,
    running,
    outgoing,
    incoming_low,
    incoming,
    first_send,
    first_recv,
    send_sems,
    recv_sems,
    gather_send,
    gather_recv,
    back_send,
    back_recv,
):
    steps = len(bits)
    depth, features = total_ref.shape[1:]
    half = features // 2
    share = depth // len(sums_refs)
    middle = list(bits[1:-1])
    orders = []
    for stream in range(STREAMS):
        turn = stream % len(middle)
        orders.append([bits[0], *middle[turn:], *middle[:turn], bits[-1]])
    barrier = pltpu.get_barrier_semaphore()
    for axis, bit in bits:
        device, _ = partner(axis, bit)
        pl.semaphore_signal(barrier, inc=1, device_id=device, device_id_type=MESH)
    greet_neighbours(barrier, steps)

    def remote(source, target, send_sem, recv_sem, device):
        return pltpu.make_async_remote_copy(
            src_ref=source,
            dst_ref=target,
            send_sem=send_sem,
            recv_sem=recv_sem,
            device_id=device,
            device_id_type=MESH,
        )

    def aligned(row):
        return pl.multiple_of(row, 16)

    def by_rows(rows, body):
        chunk = min(rows, 64)

        def step(i, carry):
            body(i * chunk, chunk)
            return carry

        lax.fori_loop(0, rows // chunk, step, 0)

    def columns(mine):
        return pl.ds(pl.multiple_of(mine * half, 128), half)

    bases = [0] * STREAMS
    started = []

    def start_step(stream, k):
        device, mine = partner(*orders[stream][k])
        if k == 0:
            copies = [
                remote(
                    source.at[pl.ds(stream * share, share), columns(1 - mine)],
                    whole_recv.at[stream, pl.ds(i * share, share)],
                    first_send.at[stream, i],
                    first_recv.at[stream, i],
                    device,
                )
                for i, source in enumerate(sums_refs)
            ]
        else:
            rows = depth >> k
            away = bases[stream] + (1 - mine) * rows
            semaphores = (send_sems.at[stream, k], recv_sems.at[stream, k])
            if k == 1:

                def cast(i, chunk):
                    own = running[stream, pl.ds(aligned(away + i), chunk), :]
                    at = pl.ds(pl.multiple_of(i, 16), chunk)
                    outgoing[stream, at, :] = own.astype(outgoing.dtype)

                by_rows(rows, cast)
                copies = [remote(outgoing.at[stream], incoming_low.at[stream], *semaphores, device)]
            else:
                place = depth // 2 - 2 * rows
                source = running.at[stream, pl.ds(aligned(away), rows)]
                target = incoming.at[stream, pl.ds(place, rows)]
                copies = [remote(source, target, *semaphores, device)]
        for copy in copies:
            copy.start()
        return copies

    def finish_step(stream, k, copies):
        _, mine = partner(*orders[stream][k])
        for copy in copies:
            copy.wait_recv()
        if k == 0:
            for i, source in enumerate(sums_refs):

                def add(row, chunk):
                    at = pl.ds(aligned(i * share + row), chunk)
                    own = source[pl.ds(aligned(stream * share + row), chunk), columns(mine)]
                    running[stream, at, :] = own + whole_recv[stream, at, :]

                by_rows(share, add)
            return
        rows = depth >> k
        bases[stream] = bases[stream] + mine * rows
        place = 0 if k == 1 else depth // 2 - 2 * rows
        source = incoming_low if k == 1 else incoming

        def add(i, chunk):
            at = pl.ds(aligned(bases[stream] + i), chunk)
            arrived = source[stream, pl.ds(aligned(place + i), chunk), :]
            running[stream, at, :] += arrived.astype(running.dtype)

        by_rows(rows, add)

    part = tile_rows(video_ref.shape[0])
    parts = video_ref.shape[0] // part
    rounds = 2 * steps

    def work(turn):
        def rows_of(i, carry):
            at = pl.ds(pl.multiple_of(i * part, 16), part)
            video = video_ref[at, :].astype(jnp.float32)
            attended = dot_nn(context_ref[at, :], w_out_ref[...])
            output_ref[at, :] = (video + attended).astype(output_ref.dtype)
            _, video_hat, inverse = normalize(video)
            back = normalize_back(dot_nt(dquery_ref[at, :], w_query_ref[...]), video_hat, inverse)
            grad = grad_ref[at, :].astype(jnp.float32)
            grad_video_ref[at, :] = (grad + back).astype(grad_video_ref.dtype)
            return carry

        first, last = turn * parts // rounds, (turn + 1) * parts // rounds
        if last > first:
            lax.fori_loop(first, last, rows_of, 0)

    live = [start_step(stream, 0) for stream in range(STREAMS)]

    def back_copy(offset):
        device, exists = neighbour(offset)
        place = offset + REACH - (offset > 0)
        return exists, remote(
            back_ref.at[place], returned_ref.at[place], back_send.at[place], back_recv.at[place], device
        )

    for offset in other_offsets():
        exists, copy = back_copy(offset)
        pl.when(exists)(copy.start)
    for offset in other_offsets():
        _, comes = neighbour(-offset)
        place = offset + REACH - (offset > 0)

        @pl.when(jnp.logical_not(comes))
        def _():
            returned_ref[place] = jnp.zeros(returned_ref.shape[1:], returned_ref.dtype)

    for k in range(steps):
        for stream in range(STREAMS):
            finish_step(stream, k, live[stream])
            started += live[stream]
            if k + 1 < steps:
                live[stream] = start_step(stream, k + 1)
        work(k)

    kept = [partner(*orders[stream][0])[1] for stream in range(STREAMS)]

    def gather_copy(stream, k):
        device, _ = partner(*orders[stream][k])
        rows = depth >> k if k else depth
        at = total_ref.at[stream, pl.ds(aligned(bases[stream]), rows), columns(kept[stream])]
        return remote(at, at, gather_send.at[stream, k], gather_recv.at[stream, k], device)

    for stream in range(STREAMS):

        def finish(i, chunk):
            at = pl.ds(aligned(bases[stream] + i), chunk)
            own = running[stream, at, :].astype(total_ref.dtype)
            total_ref[stream, at, columns(kept[stream])] = own

        by_rows(depth >> (steps - 1), finish)
        live[stream] = gather_copy(stream, steps - 1)
        live[stream].start()
    for k in reversed(range(steps)):
        work(2 * steps - 1 - k)
        for stream in range(STREAMS):
            _, mine = partner(*orders[stream][k])
            live[stream].wait_recv()
            started.append(live[stream])
            if k > 0:
                bases[stream] = bases[stream] - mine * (depth >> k)
                live[stream] = gather_copy(stream, k - 1)
                live[stream].start()
    for copy in started:
        copy.wait_send()
    for offset in other_offsets():
        exists, copy = back_copy(offset)
        _, comes = neighbour(-offset)
        pl.when(exists)(copy.wait_send)
        pl.when(comes)(copy.wait_recv)


def sum_devices(sums, back, context, dquery, video, grad, w_out, w_query):
    bits = [
        (axis, bit)
        for axis in ("audio", "frame")
        for bit in range((lax.axis_size(axis) - 1).bit_length())
    ]
    steps = len(bits)
    rows, features = sums[0].shape
    depth = len(sums) * rows // STREAMS
    half = features // 2
    vmem = pl.BlockSpec(memory_space=pltpu.VMEM)
    return pl.pallas_call(
        functools.partial(sum_kernel, bits),
        in_specs=[[vmem] * len(sums)] + [vmem] * 7,
        out_specs=[vmem] * 4,
        out_shape=[
            jax.ShapeDtypeStruct((STREAMS, depth, features), jnp.bfloat16),
            jax.ShapeDtypeStruct(back.shape, back.dtype),
            jax.ShapeDtypeStruct(video.shape, video.dtype),
            jax.ShapeDtypeStruct(grad.shape, grad.dtype),
        ],
        scratch_shapes=[
            pltpu.VMEM((STREAMS, depth, half), jnp.float32),
            pltpu.VMEM((STREAMS, depth, half), jnp.float32),
            pltpu.VMEM((STREAMS, depth // 2, half), jnp.bfloat16),
            pltpu.VMEM((STREAMS, depth // 2, half), jnp.bfloat16),
            pltpu.VMEM((STREAMS, depth // 2, half), jnp.float32),
            pltpu.SemaphoreType.DMA((STREAMS, len(sums))),
            pltpu.SemaphoreType.DMA((STREAMS, len(sums))),
            pltpu.SemaphoreType.DMA((STREAMS, steps)),
            pltpu.SemaphoreType.DMA((STREAMS, steps)),
            pltpu.SemaphoreType.DMA((STREAMS, steps)),
            pltpu.SemaphoreType.DMA((STREAMS, steps)),
            pltpu.SemaphoreType.DMA((2 * REACH,)),
            pltpu.SemaphoreType.DMA((2 * REACH,)),
        ],
        compiler_params=pltpu.CompilerParams(
            collective_id=2, has_side_effects=True, vmem_limit_bytes=52 * 1024 * 1024
        ),
        name="sum_devices",
    )(sums, back, context, dquery, video, grad, w_out, w_query)


def normalize(row_block):
    centred = row_block.astype(jnp.float32)
    centred = centred - jnp.mean(centred, axis=-1, keepdims=True)
    inverse = lax.rsqrt(jnp.mean(centred * centred, axis=-1, keepdims=True) + 1e-05)
    normed_hat = centred * inverse
    return (normed_hat.astype(jnp.bfloat16), normed_hat, inverse)


def normalize_back(gradient, normed_hat, inverse):
    first = jnp.mean(gradient, axis=-1, keepdims=True)
    second = jnp.mean(gradient * normed_hat, axis=-1, keepdims=True)
    return inverse * (gradient - first - normed_hat * second)


def dot_nt(left, right):
    return lax.dot_general(left, right, (((1,), (1,)), ((), ())), preferred_element_type=jnp.float32)


def dot_nn(left, right):
    return jnp.dot(left, right, preferred_element_type=jnp.float32)


def per_head(reduced, low, high):
    rows = low.shape[0]
    return jnp.concatenate(
        [
            jnp.broadcast_to(reduced(low, axis=1, keepdims=True), (rows, TILE)),
            jnp.broadcast_to(reduced(high, axis=1, keepdims=True), (rows, TILE)),
        ],
        axis=1,
    )


def attention_kernel(
    tiles_ref,
    count_ref,
    fill_ref,
    query_ref,
    dcontext_ref,
    keys_ref,
    values_ref,
    context_ref,
    dquery_ref,
    dkeys_ref,
    dvalues_ref,
    pair_keys,
    pair_values,
    sum_keys,
    sum_values,
    query_pad,
    dcontext_pad,
    scores_scr,
    dattention_scr,
    low_scr,
    dscores_scr,
):
    frame = pl.program_id(1)
    patch = query_ref.shape[1]
    padded, width = query_pad.shape
    half = width // 2
    listed = tiles_ref.shape[1]
    window = pair_keys.shape[0]
    scale = 1.0 / math.sqrt(half)

    @pl.when(frame == 0)
    def _():
        first = lax.broadcasted_iota(jnp.int32, (TILE, width), 1) < half
        for tile in range(window):
            for source, target in ((keys_ref, pair_keys), (values_ref, pair_values)):
                block = source[tile * TILE : (tile + 1) * TILE, :]
                zero = jnp.zeros_like(block)
                target[tile, :TILE, :] = jnp.where(first, block, zero)
                target[tile, TILE:, :] = jnp.where(first, zero, block)
        sum_keys[...] = jnp.zeros_like(sum_keys)
        sum_values[...] = jnp.zeros_like(sum_values)
        for pad in (query_pad, dcontext_pad):
            pad[padded - 16 :, :] = jnp.zeros((16, width), pad.dtype)

    query_pad[:patch, :] = query_ref[0] * jnp.asarray(scale, query_ref.dtype)
    dcontext_pad[:patch, :] = dcontext_ref[0]
    count = count_ref[frame]

    def work(slots):
        query = query_pad[...]
        dcontext = dcontext_pad[...]
        query_t = query.T
        dcontext_t = dcontext.T
        lane = lax.rem(lax.broadcasted_iota(jnp.int32, (1, 2 * TILE), 1), TILE)
        places, biases = [], []
        for j in range(slots):
            place = tiles_ref[frame, j]
            seen = jnp.where(j < count, fill_ref[place], 0)
            places.append(place)
            biases.append(jnp.where(lane < seen, 0.0, -1e30))
        for j in range(slots):
            columns = slice(j * 2 * TILE, (j + 1) * 2 * TILE)
            scores_scr[:, columns] = dot_nt(query, pair_keys[places[j]]) + biases[j]
            dattention_scr[:, columns] = dot_nt(dcontext, pair_values[places[j]])
        for start in range(0, padded, 16):
            rows = slice(start, start + 16)
            scores = [scores_scr[rows, j * 2 * TILE : (j + 1) * 2 * TILE] for j in range(slots)]
            highest = functools.reduce(jnp.maximum, scores)
            highest = per_head(jnp.max, highest[:, :TILE], highest[:, TILE:])
            exponent = [jnp.exp(part - highest) for part in scores]
            total = functools.reduce(jnp.add, exponent)
            inverse = 1.0 / per_head(jnp.sum, total[:, :TILE], total[:, TILE:])
            attention = [part * inverse for part in exponent]
            dattention = [
                dattention_scr[rows, j * 2 * TILE : (j + 1) * 2 * TILE] for j in range(slots)
            ]
            weighed = functools.reduce(
                jnp.add, [a * b for a, b in zip(attention, dattention)]
            )
            weighed = per_head(jnp.sum, weighed[:, :TILE], weighed[:, TILE:])
            for j in range(slots):
                columns = slice(j * 2 * TILE, (j + 1) * 2 * TILE)
                low_scr[rows, columns] = attention[j].astype(jnp.bfloat16)
                dscores_scr[rows, columns] = (
                    attention[j] * (dattention[j] - weighed)
                ).astype(jnp.bfloat16)
        context = jnp.zeros((padded, width), jnp.float32)
        dquery = jnp.zeros((padded, width), jnp.float32)
        for j in range(slots):
            columns = slice(j * 2 * TILE, (j + 1) * 2 * TILE)
            low, dscores = low_scr[:, columns], dscores_scr[:, columns]
            context += dot_nn(low, pair_values[places[j]])
            dquery += dot_nn(dscores, pair_keys[places[j]])
            sum_keys[places[j]] += dot_nn(query_t, dscores)
            sum_values[places[j]] += dot_nn(dcontext_t, low)
        context_ref[0] = context[:patch].astype(context_ref.dtype)
        dquery_ref[0] = (dquery[:patch] * scale).astype(dquery_ref.dtype)

    least = 0
    for slots in sorted({min(size, listed) for size in SIZES} | {listed}):
        pl.when((count > least) & (count <= slots))(functools.partial(work, slots))
        least = slots

    @pl.when(frame == pl.num_programs(1) - 1)
    def _():
        for total, target in ((sum_keys, dkeys_ref), (sum_values, dvalues_ref)):
            for tile in range(window):
                columns = slice(tile * TILE, (tile + 1) * TILE)
                target[:half, columns] = total[tile, :half, :TILE].astype(target.dtype)
                target[half:, columns] = total[tile, half:, TILE:].astype(target.dtype)


def attend(local_block, count_block, fill_window, query, dcontext, key_window, value_window):
    frames, patch, width = query.shape
    slots = key_window.shape[0]
    window = slots // TILE
    listed = local_block.shape[1]
    pair = 2 * TILE // 2
    padded = -(-patch // 16) * 16
    frame_spec = pl.BlockSpec((1, patch, pair), lambda p, f, *_: (f, 0, p))
    window_spec = pl.BlockSpec((slots, pair), lambda p, f, *_: (0, p))
    sums_spec = pl.BlockSpec((pair, slots), lambda p, f, *_: (p, 0))
    work = frames * patch * width * listed * TILE
    return pl.pallas_call(
        attention_kernel,
        grid_spec=pltpu.PrefetchScalarGridSpec(
            num_scalar_prefetch=3,
            grid=(width // pair, frames),
            in_specs=[frame_spec, frame_spec, window_spec, window_spec],
            out_specs=[frame_spec, frame_spec, sums_spec, sums_spec],
            scratch_shapes=[
                pltpu.VMEM((window, 2 * TILE, pair), jnp.bfloat16),
                pltpu.VMEM((window, 2 * TILE, pair), jnp.bfloat16),
                pltpu.VMEM((window, pair, 2 * TILE), jnp.float32),
                pltpu.VMEM((window, pair, 2 * TILE), jnp.float32),
                pltpu.VMEM((padded, pair), jnp.bfloat16),
                pltpu.VMEM((padded, pair), jnp.bfloat16),
                pltpu.VMEM((padded, listed * 2 * TILE), jnp.float32),
                pltpu.VMEM((padded, listed * 2 * TILE), jnp.float32),
                pltpu.VMEM((padded, listed * 2 * TILE), jnp.bfloat16),
                pltpu.VMEM((padded, listed * 2 * TILE), jnp.bfloat16),
            ],
        ),
        out_shape=[
            jax.ShapeDtypeStruct(query.shape, jnp.bfloat16),
            jax.ShapeDtypeStruct(query.shape, jnp.bfloat16),
            jax.ShapeDtypeStruct((width, slots), jnp.bfloat16),
            jax.ShapeDtypeStruct((width, slots), jnp.bfloat16),
        ],
        compiler_params=pltpu.CompilerParams(vmem_limit_bytes=40 * 1024 * 1024),
        cost_estimate=pl.CostEstimate(
            flops=48 * work,
            bytes_accessed=8 * frames * patch * width + 8 * slots * width,
            transcendentals=work // 64,
        ),
        name="attend",
    )(local_block, count_block, fill_window, query, dcontext, key_window, value_window)


def per_device(
    video,
    audio,
    w_query,
    w_key,
    w_value,
    w_out,
    grad_output,
    intersection_tiles,
    intersection_count,
    tile_fill,
):
    tiles_dev = tile_fill.shape[0]
    window_tiles = (2 * REACH + 1) * tiles_dev
    frames = intersection_count.shape[0]
    features = video.shape[1]
    contract_rows = (((0,), (0,)), ((), ()))
    video_normed, _, _ = normalize(video)
    audio_normed, audio_hat, audio_inverse = normalize(audio)
    device_index = lax.axis_index(("frame", "audio"))
    fill_rows = jnp.pad(tile_fill[None, :], ((0, 7), (0, TILE - tiles_dev)))
    normed_window, fill_window, query, dcontext = gather_halo(
        audio_normed, fill_rows, video_normed, grad_output, w_query, w_out
    )
    normed_window = normed_window.reshape(-1, features)
    fill_window = fill_window[:, 0, :tiles_dev].reshape(-1)
    local_block = jnp.clip(
        intersection_tiles - (device_index - REACH) * tiles_dev, 0, window_tiles - 1
    )
    key_window = dot_nn(normed_window, w_key).astype(jnp.bfloat16)
    value_window = dot_nn(normed_window, w_value).astype(jnp.bfloat16)
    context, dquery, dkeys, dvalues = attend(
        local_block,
        intersection_count,
        fill_window,
        query.reshape(frames, -1, features),
        dcontext.reshape(frames, -1, features),
        key_window,
        value_window,
    )
    context = context.reshape(-1, features)
    dquery = dquery.reshape(-1, features)
    window_rows = (((0,), (1,)), ((), ()))
    partial_sums = [
        lax.dot_general(left, right, dims, preferred_element_type=jnp.float32)
        for left, right, dims in (
            (video_normed, dquery, contract_rows),
            (normed_window, dkeys, window_rows),
            (normed_window, dvalues, window_rows),
            (context, grad_output, contract_rows),
        )
    ]
    dnormed_window = lax.dot_general(
        dkeys, w_key, (((0,), (1,)), ((), ())), preferred_element_type=jnp.float32
    ) + lax.dot_general(
        dvalues, w_value, (((0,), (1,)), ((), ())), preferred_element_type=jnp.float32
    )
    dnormed_window = dnormed_window.reshape(2 * REACH + 1, -1, features)
    back = jnp.concatenate([dnormed_window[:REACH], dnormed_window[REACH + 1 :]])
    total, returned, output, grad_video = sum_devices(
        partial_sums,
        back.astype(jnp.bfloat16),
        context,
        dquery,
        video,
        grad_output,
        w_out,
        w_query,
    )
    daudio_normed = dnormed_window[REACH] + jnp.sum(returned.astype(jnp.float32), axis=0)
    grad_audio = normalize_back(daudio_normed, audio_hat, audio_inverse).astype(jnp.bfloat16)
    total = total.reshape(STREAMS, len(partial_sums), -1, features).astype(jnp.float32)
    total = [total[:, i].reshape(-1, features) for i in range(len(partial_sums))]
    return (output, grad_video, grad_audio, total[0], total[1], total[2], total[3])


def solution(mesh):
    in_specs = (
        P(("frame", "audio"), None),
        P(("frame", "audio"), None),
        P(),
        P(),
        P(),
        P(),
        P(("frame", "audio"), None),
        P(("frame", "audio"), None),
        P(("frame", "audio")),
        P(("frame", "audio")),
    )
    out_specs = (
        P(("frame", "audio"), None),
        P(("frame", "audio"), None),
        P(("frame", "audio"), None),
        P(),
        P(),
        P(),
        P(),
    )
    return jax.shard_map(
        per_device, mesh=mesh, in_specs=in_specs, out_specs=out_specs, check_vma=False
    )
```

profile of v0, /device:TPU:0, one launch (start us, length us, event | category | flops | bytes accessed | tf_op | source)
XLA Modules:
  0.0 247.6 jit_solution(12273385764681798147)
XLA Ops:
  0.7 1.3 convert_reduce_fusion.2
  2.0 1.2 fusion.13
  3.2 0.7 subtract_clamp_fusion.tiles_ref
  3.9 0.7 pad.4.fill_ref
  4.6 1.5 convert_reduce_fusion.1
  8.1 26.3 %gather_halo.1 = (bf16[5,256,768]{2,1,0:T(8,128)(2,1)S(1)}, s32[5,8,128]{2,1,0:T(8,128)S(1)}, bf16[784,768]{1,0:T(8,128)(2,1)S(1)}, bf16[784,768]{1,0:T(8,128)(2,1)S(1)}) custom-call(bf16[256,768]{1,0:T(8,128)(2,1)S(1)} %fusion.8.rows_ref, s32[8,128]{1,0:T(8,128)S(1)} %pad.4.fill_ref, bf16[784,768]{1,0:T(8,128)(2,1)S(1)} %fusion.3.normed_ref, ...), custom_call_target="tpu_custom_call" | custom-call | tf_op jit(solution)/shard_map/gather_halo/pallas_call | solution.py:119
  34.5 1.0 copy-done.10
  35.5 1.3 copy-done.11
  36.9 2.2 reshape.71.query_ref
  39.1 1.1 reshape.72.dcontext_ref
  40.2 3.4 %convolution_convert_fusion.values_ref = bf16[1280,768]{1,0:T(8,128)(2,1)S(1)} fusion(bf16[1280,768]{1,0:T(8,128)(2,1)} %bitcast.26, bf16[768,768]{1,0:T(8,128)(2,1)S(1)} %copy-done), kind=kOutput, calls=%fused_computation.1 | convolution fusion | flops 1510932480 | bytes 5111808 | tf_op jit(solution)/shard_map/dot_general | solution.py:428
  43.7 1.7 convolution_convert_fusion.1.keys_ref
  45.4 41.2 %attend.1 = (bf16[4,196,768]{2,1,0:T(8,128)(2,1)S(1)}, bf16[4,196,768]{2,1,0:T(8,128)(2,1)S(1)}, bf16[768,1280]{1,0:T(8,128)(2,1)S(1)}, bf16[768,1280]{1,0:T(8,128)(2,1)S(1)}) custom-call(s32[4,8]{1,0:T(4,128)S(1)} %subtract_clamp_fusion.tiles_ref, s32[4]{0:T(128)S(1)} %copy-done.14, s32[10]{0:T(128)S(1)} %reshape_squeeze.15.fill_ref, ...), custom_call_target="tpu_custom_call" | custom-call | flops 29595009024 | bytes 12681216 | tf_op jit(solution)/shard_map/attend/pallas_call | solution.py:566
  86.6 1.0 copy-done.6
  87.6 1.0 copy-done.9
  88.6 1.3 copy-done.15
  89.9 2.2 reshape.74.dquery_ref
  92.1 4.5 %fusion.18.sums_refs_0_ = f32[768,768]{1,0:T(8,128)} fusion(bf16[784,768]{1,0:T(8,128)(2,1)} %copy-done.2, bf16[784,768]{1,0:T(8,128)(2,1)} %reshape.74.dquery_ref), kind=kOutput, calls=%fused_computation.36 | convolution fusion | flops 924844032 | bytes 4767744 | tf_op jit(solution)/shard_map/dot_general | solution.py:646
  96.6 2.2 reshape.75.context_ref
  98.8 4.6 %fusion.21.sums_refs_3_ = f32[768,768]{1,0:T(8,128)} fusion(bf16[784,768]{1,0:T(8,128)(2,1)} %reshape.75.context_ref, bf16[784,768]{1,0:T(8,128)(2,1)} %grad_ref.3), kind=kOutput, calls=%fused_computation.39 | convolution fusion | flops 924844032 | bytes 4767744 | tf_op jit(solution)/shard_map/dot_general | solution.py:646
  103.5 3.2 %fusion.19.sums_refs_1_ = f32[768,768]{1,0:T(8,128)} fusion(bf16[1280,768]{1,0:T(8,128)(2,1)S(1)} %bitcast.28, bf16[768,1280]{1,0:T(8,128)(2,1)S(1)} %copy-done.16), kind=kOutput, calls=%fused_computation.37 | convolution fusion | flops 1509949440 | bytes 6291456 | tf_op jit(solution)/shard_map/dot_general | solution.py:646
  106.6 3.2 %fusion.20.sums_refs_2_ = f32[768,768]{1,0:T(8,128)} fusion(bf16[1280,768]{1,0:T(8,128)(2,1)S(1)} %bitcast.29, bf16[768,1280]{1,0:T(8,128)(2,1)S(1)} %get-tuple-element.25), kind=kOutput, calls=%fused_computation.38 | convolution fusion | flops 1509949440 | bytes 6291456 | tf_op jit(solution)/shard_map/dot_general | solution.py:646
  109.8 1.8 fusion.22
  111.5 1.8 fusion.17
  113.5 1.3 pad_maximum_fusion.back_ref
  115.3 122.5 %sum_devices.1 = (bf16[3,1024,768]{2,1,0:T(8,128)(2,1)}, bf16[4,256,768]{2,1,0:T(8,128)(2,1)}, bf16[784,768]{1,0:T(8,128)(2,1)}, bf16[784,768]{1,0:T(8,128)(2,1)}) custom-call(f32[768,768]{1,0:T(8,128)} %fusion.18.sums_refs_0_, f32[768,768]{1,0:T(8,128)} %fusion.19.sums_refs_1_, f32[768,768]{1,0:T(8,128)} %fusion.20.sums_refs_2_, ...), custom_call_target="tpu_custom_call" | custom-call | tf_op jit(solution)/shard_map/sum_devices/pallas_call | solution.py:377
  237.8 1.9 convert_reduce_fusion
  240.0 1.0 fusion.12
  241.0 3.9 %fusion.15 = (f32[3,1,256,768]{3,2,1,0:T(8,128)}, f32[3,1,256,768]{3,2,1,0:T(8,128)}, f32[3,1,256,768]{3,2,1,0:T(8,128)}, f32[3,1,256,768]{3,2,1,0:T(8,128)}) fusion(bf16[3,4,256,768]{3,2,1,0:T(8,128)(2,1)S(1)} %bitcast.30), kind=kLoop, calls=%fused_computation.33 | loop fusion | bytes 18874368 | tf_op jit(solution)/shard_map/slice | solution.py:674
  244.9 1.0 copy.19
  245.9 0.7 copy-done.20
  246.6 1.0 copy.20
  (54 shorter events, 3.0 us)
Async XLA Ops:
  0.6 39.6 %copy-start = (bf16[768,768]{1,0:T(8,128)(2,1)S(1)}, bf16[768,768]{1,0:T(8,128)(2,1)}, u32[]{:S(2)}) copy-start(bf16[768,768]{1,0:T(8,128)(2,1)} %param.14) | copy-start | bytes 3538948
  0.6 6.0 %copy-start.19 = (bf16[256,768]{1,0:T(8,128)(2,1)S(1)}, bf16[256,768]{1,0:T(8,128)(2,1)}, u32[]{:S(2)}) copy-start(bf16[256,768]{1,0:T(8,128)(2,1)} %param.11) | copy-start | bytes 1179652
  0.7 5.4 %copy-start.17 = (bf16[784,768]{1,0:T(8,128)(2,1)S(1)}, bf16[784,768]{1,0:T(8,128)(2,1)}, u32[]{:S(2)}) copy-start(bf16[784,768]{1,0:T(8,128)(2,1)} %video_ref.1) | copy-start | bytes 3612676
  6.1 1.3 copy-start.1
  6.1 1.6 copy-start.3
  6.1 2.0 copy-start.4
  8.1 26.3 %copy-start.2 = (bf16[784,768]{1,0:T(8,128)(2,1)}, bf16[784,768]{1,0:T(8,128)(2,1)S(1)}, u32[]{:S(2)}) copy-start(bf16[784,768]{1,0:T(8,128)(2,1)S(1)} %fusion.3.normed_ref) | copy-start | bytes 3612676
  34.5 1.0 copy-start.10
  35.5 1.3 copy-start.11
  40.2 3.4 %copy-start.12 = (bf16[5,256,768]{2,1,0:T(8,128)(2,1)S(1)}, bf16[5,256,768]{2,1,0:T(8,128)(2,1)}, u32[]{:S(2)}) copy-start(bf16[5,256,768]{2,1,0:T(8,128)(2,1)} %copy-done.11) | copy-start | bytes 5898244
  40.2 3.4 %copy-start.22 = (bf16[768,768]{1,0:T(8,128)(2,1)S(1)}, bf16[768,768]{1,0:T(8,128)(2,1)}, u32[]{:S(2)}) copy-start(bf16[768,768]{1,0:T(8,128)(2,1)} %param.13) | copy-start | bytes 3538948
  43.6 1.7 copy-start.7
  43.7 1.7 copy-start.8
  43.7 1.7 copy-start.14
  86.6 1.0 copy-start.6
  87.6 1.0 copy-start.9
  88.6 1.3 copy-start.15
  98.8 4.6 %copy-start.13 = (bf16[5,256,768]{2,1,0:T(8,128)(2,1)S(1)}, bf16[5,256,768]{2,1,0:T(8,128)(2,1)}, u32[]{:S(2)}) copy-start(bf16[5,256,768]{2,1,0:T(8,128)(2,1)} %copy-done.11) | copy-start | bytes 5898244
  98.8 4.6 %copy-start.16 = (bf16[768,1280]{1,0:T(8,128)(2,1)S(1)}, bf16[768,1280]{1,0:T(8,128)(2,1)}, u32[]{:S(2)}) copy-start(bf16[768,1280]{1,0:T(8,128)(2,1)} %copy-done.15) | copy-start | bytes 5898244
  106.6 3.2 %copy-start.23 = (bf16[768,768]{1,0:T(8,128)(2,1)S(1)}, bf16[768,768]{1,0:T(8,128)(2,1)}, u32[]{:S(2)}) copy-start(bf16[768,768]{1,0:T(8,128)(2,1)} %param.13) | copy-start | bytes 3538948
  113.5 1.7 copy-start.5
  237.8 3.3 %copy-start.18 = (bf16[3,1024,768]{2,1,0:T(8,128)(2,1)S(1)}, bf16[3,1024,768]{2,1,0:T(8,128)(2,1)}, u32[]{:S(2)}) copy-start(bf16[3,1024,768]{2,1,0:T(8,128)(2,1)} %get-tuple-element.30) | copy-start | bytes 14155780
  241.0 3.9 %copy-start.21 = (bf16[784,768]{1,0:T(8,128)(2,1)S(1)}, bf16[784,768]{1,0:T(8,128)(2,1)}, u32[]{:S(2)}) copy-start(bf16[784,768]{1,0:T(8,128)(2,1)} %get-tuple-element.50) | copy-start | bytes 3612676
  244.9 1.7 copy-start.20
where the time goes:
time: 248 us
  Pallas kernels  190 us (77%)
  matrix products  24.1 us (10%)
  local copies, waits for them, and re-layouts  22.2 us (9%)
  other arithmetic  10.4 us (4%)
    pallas_call x1, Pallas kernels, sum_devices(): pl.pallas_call(functools.partial(sum_kernel, bits), in_specs=[[vmem] * le...  123 us
    pallas_call x1, Pallas kernels, attend(): pl.pallas_call(attention_kernel, grid_spec=pltpu.PrefetchScalarGridSpec(n...  41.2 us
    pallas_call x1, Pallas kernels, gather_halo(): pl.pallas_call(halo_kernel, in_specs=[vmem] * 6, out_specs=[vmem] * 4, ou...  26.3 us
    dot_general x4, matrix products, per_device(): lax.dot_general(left, right, dims, preferred_element_type=jnp.float32)  15.4 us
    unnamed x50, local copies, waits for them, and re-layouts  9.74 us
    dot_general x2, matrix products, dot_nn(): return jnp.dot(left, right, preferred_element_type=jnp.float32)  5.09 us

commit v1 on v0

--- a/solution.py
+++ b/solution.py
@@ -13,7 +13,7 @@
 REACH = 2
 STREAMS = 3
 MESH = pl.DeviceIdType.MESH
-SIZES = (2, 4, 6, 8)
+SIZES = (1, 2, 3, 4, 5, 6, 7, 8)
 
 
 def neighbour(distance):
@@ -89,15 +89,12 @@
             window_ref[place] = jnp.zeros(rows_ref.shape, rows_ref.dtype)
             fills_ref[place] = jnp.zeros(fill_ref.shape, fill_ref.dtype)
 
-    part = tile_rows(normed_ref.shape[0])
-
-    def project(i, carry):
-        at = pl.ds(pl.multiple_of(i * part, 16), part)
-        query_ref[at, :] = dot_nn(normed_ref[at, :], w_query_ref[...]).astype(query_ref.dtype)
-        dcontext_ref[at, :] = dot_nt(grad_ref[at, :], w_out_ref[...]).astype(dcontext_ref.dtype)
-        return carry
-
-    lax.fori_loop(0, normed_ref.shape[0] // part, project, 0)
+    frames, patch = query_ref.shape[:2]
+    for frame in range(frames):
+        at = slice(frame * patch, (frame + 1) * patch)
+        query_ref[frame] = dot_nn(normed_ref[at, :], w_query_ref[...]).astype(query_ref.dtype)
+        dcontext_ref[frame] = dot_nt(grad_ref[at, :], w_out_ref[...]).astype(dcontext_ref.dtype)
+
     for offset in other_offsets():
         exists, pair = copies(offset)
         _, comes = neighbour(-offset)
@@ -113,7 +110,7 @@
                 copy.wait_recv()
 
 
-def gather_halo(rows, fill, normed, grad, w_query, w_out):
+def gather_halo(rows, fill, normed, grad, w_query, w_out, frames):
     vmem = pl.BlockSpec(memory_space=pltpu.VMEM)
     spread = 2 * REACH + 1
     return pl.pallas_call(
@@ -123,8 +120,8 @@
         out_shape=[
             jax.ShapeDtypeStruct((spread, *rows.shape), rows.dtype),
             jax.ShapeDtypeStruct((spread, *fill.shape), fill.dtype),
-            jax.ShapeDtypeStruct(normed.shape, normed.dtype),
-            jax.ShapeDtypeStruct(grad.shape, grad.dtype),
+            jax.ShapeDtypeStruct((frames, normed.shape[0] // frames, normed.shape[1]), normed.dtype),
+            jax.ShapeDtypeStruct((frames, grad.shape[0] // frames, grad.shape[1]), grad.dtype),
         ],
         scratch_shapes=[
             pltpu.SemaphoreType.DMA((2, spread)),
@@ -621,7 +618,7 @@
     device_index = lax.axis_index(("frame", "audio"))
     fill_rows = jnp.pad(tile_fill[None, :], ((0, 7), (0, TILE - tiles_dev)))
     normed_window, fill_window, query, dcontext = gather_halo(
-        audio_normed, fill_rows, video_normed, grad_output, w_query, w_out
+        audio_normed, fill_rows, video_normed, grad_output, w_query, w_out, frames
     )
     normed_window = normed_window.reshape(-1, features)
     fill_window = fill_window[:, 0, :tiles_dev].reshape(-1)
@@ -634,8 +631,8 @@
         local_block,
         intersection_count,
         fill_window,
-        query.reshape(frames, -1, features),
-        dcontext.reshape(frames, -1, features),
+        query,
+        dcontext,
         key_window,
         value_window,
     )

time: 248 us -> 237 us (0.956)
  Pallas kernels: 190 us -> 182 us
    pallas_call x1, Pallas kernels: 123 us -> 116 us  [sum_devices(): pl.pallas_call(functools.partial(sum_kernel, bits), in_specs=[[vmem] * le...]
    reshape x2 -> x0, local copies, waits for them, and re-layouts: 3.36 us -> none  [the longest x1 2.22 us: per_device(): query.reshape(frames, -1, features)]
where the time goes in v1:
time: 237 us; the launch traced here: 235 us
  Pallas kernels  182 us (77%)
  matrix products  22.4 us (9%)
  local copies, waits for them, and re-layouts  20 us (8%)
  other arithmetic  10.4 us (4%)
    pallas_call x1, Pallas kernels, sum_devices(): pl.pallas_call(functools.partial(sum_kernel, bits), in_specs=[[vmem] * le...  116 us
    pallas_call x1, Pallas kernels, attend(): pl.pallas_call(attention_kernel, grid_spec=pltpu.PrefetchScalarGridSpec(n...  39.3 us
    pallas_call x1, Pallas kernels, gather_halo(): pl.pallas_call(halo_kernel, in_specs=[vmem] * 6, out_specs=[vmem] * 4, ou...  26.3 us
    dot_general x4, matrix products, per_device(): lax.dot_general(left, right, dims, preferred_element_type=jnp.float32)  15.4 us
    unnamed x50, local copies, waits for them, and re-layouts  9.5 us

profile of v1, /device:TPU:0, one launch (start us, length us, event | category | flops | bytes accessed | tf_op | source)
XLA Modules:
  0.0 235.5 jit_solution(1107441002507289661)
XLA Ops:
  0.7 1.3 convert_reduce_fusion.2
  2.0 1.2 fusion.13
  3.2 0.7 subtract_clamp_fusion.tiles_ref
  3.9 0.7 pad.4.fill_ref
  4.6 1.5 convert_reduce_fusion.1
  8.1 26.3 %gather_halo.1 = (bf16[5,256,768]{2,1,0:T(8,128)(2,1)S(1)}, s32[5,8,128]{2,1,0:T(8,128)S(1)}, bf16[4,196,768]{2,1,0:T(8,128)(2,1)S(1)}, bf16[4,196,768]{2,1,0:T(8,128)(2,1)S(1)}) custom-call(bf16[256,768]{1,0:T(8,128)(2,1)S(1)} %fusion.8.rows_ref, s32[8,128]{1,0:T(8,128)S(1)} %pad.4.fill_ref, bf16[784,768]{1,0:T(8,128)(2,1)S(1)} %fusion.3.normed_ref, ...), custom_call_target="tpu_custom_call" | custom-call | tf_op jit(solution)/shard_map/gather_halo/pallas_call | solution.py:116
  34.5 1.0 copy-done.10
  35.5 1.0 copy-done.12
  36.5 0.6 slice_reduce_fusion
  37.2 0.8 reshape_squeeze.15.fill_ref
  38.0 1.7 convolution_convert_fusion.values_ref
  39.7 1.7 convolution_convert_fusion.1.keys_ref
  41.5 39.3 %attend.1 = (bf16[4,196,768]{2,1,0:T(8,128)(2,1)S(1)}, bf16[4,196,768]{2,1,0:T(8,128)(2,1)S(1)}, bf16[768,1280]{1,0:T(8,128)(2,1)S(1)}, bf16[768,1280]{1,0:T(8,128)(2,1)S(1)}) custom-call(s32[4,8]{1,0:T(4,128)S(1)} %subtract_clamp_fusion.tiles_ref, s32[4]{0:T(128)S(1)} %copy-done.14, s32[10]{0:T(128)S(1)} %reshape_squeeze.15.fill_ref, ...), custom_call_target="tpu_custom_call" | custom-call | flops 29595009024 | bytes 12681216 | tf_op jit(solution)/shard_map/attend/pallas_call | solution.py:563
  80.8 1.0 copy-done.6
  81.8 1.0 copy-done.7
  82.8 1.3 copy-done.15
  84.1 2.2 reshape.66.dquery_ref
  86.3 4.5 %fusion.18.sums_refs_0_ = f32[768,768]{1,0:T(8,128)} fusion(bf16[784,768]{1,0:T(8,128)(2,1)} %copy-done.2, bf16[784,768]{1,0:T(8,128)(2,1)} %reshape.66.dquery_ref), kind=kOutput, calls=%fused_computation.36 | convolution fusion | flops 924844032 | bytes 4767744 | tf_op jit(solution)/shard_map/dot_general | solution.py:643
  90.8 2.2 reshape.67.context_ref
  93.0 4.6 %fusion.21.sums_refs_3_ = f32[768,768]{1,0:T(8,128)} fusion(bf16[784,768]{1,0:T(8,128)(2,1)} %reshape.67.context_ref, bf16[784,768]{1,0:T(8,128)(2,1)} %grad_ref.3), kind=kOutput, calls=%fused_computation.39 | convolution fusion | flops 924844032 | bytes 4767744 | tf_op jit(solution)/shard_map/dot_general | solution.py:643
  97.6 3.2 %fusion.19.sums_refs_1_ = f32[768,768]{1,0:T(8,128)} fusion(bf16[1280,768]{1,0:T(8,128)(2,1)S(1)} %bitcast.28, bf16[768,1280]{1,0:T(8,128)(2,1)S(1)} %copy-done.16), kind=kOutput, calls=%fused_computation.37 | convolution fusion | flops 1509949440 | bytes 6291456 | tf_op jit(solution)/shard_map/dot_general | solution.py:643
  100.8 3.2 %fusion.20.sums_refs_2_ = f32[768,768]{1,0:T(8,128)} fusion(bf16[1280,768]{1,0:T(8,128)(2,1)S(1)} %bitcast.29, bf16[768,1280]{1,0:T(8,128)(2,1)S(1)} %get-tuple-element.25), kind=kOutput, calls=%fused_computation.38 | convolution fusion | flops 1509949440 | bytes 6291456 | tf_op jit(solution)/shard_map/dot_general | solution.py:643
  103.9 1.8 fusion.22
  105.7 1.8 fusion.17
  107.7 1.3 pad_maximum_fusion.back_ref
  109.4 116.2 %sum_devices.1 = (bf16[3,1024,768]{2,1,0:T(8,128)(2,1)}, bf16[4,256,768]{2,1,0:T(8,128)(2,1)}, bf16[784,768]{1,0:T(8,128)(2,1)}, bf16[784,768]{1,0:T(8,128)(2,1)}) custom-call(f32[768,768]{1,0:T(8,128)} %fusion.18.sums_refs_0_, f32[768,768]{1,0:T(8,128)} %fusion.19.sums_refs_1_, f32[768,768]{1,0:T(8,128)} %fusion.20.sums_refs_2_, ...), custom_call_target="tpu_custom_call" | custom-call | tf_op jit(solution)/shard_map/sum_devices/pallas_call | solution.py:374
  225.6 1.9 convert_reduce_fusion
  227.8 1.0 fusion.12
  228.9 3.9 %fusion.15 = (f32[3,1,256,768]{3,2,1,0:T(8,128)}, f32[3,1,256,768]{3,2,1,0:T(8,128)}, f32[3,1,256,768]{3,2,1,0:T(8,128)}, f32[3,1,256,768]{3,2,1,0:T(8,128)}) fusion(bf16[3,4,256,768]{3,2,1,0:T(8,128)(2,1)S(1)} %bitcast.30), kind=kLoop, calls=%fused_computation.33 | loop fusion | bytes 18874368 | tf_op jit(solution)/shard_map/slice | solution.py:671
  232.8 1.0 copy.19
  233.8 0.7 copy-done.20
  234.5 1.0 copy.20
  (52 shorter events, 2.9 us)
Async XLA Ops:
  0.6 37.3 %copy-start = (bf16[768,768]{1,0:T(8,128)(2,1)S(1)}, bf16[768,768]{1,0:T(8,128)(2,1)}, u32[]{:S(2)}) copy-start(bf16[768,768]{1,0:T(8,128)(2,1)} %param.14) | copy-start | bytes 3538948
  0.6 6.0 %copy-start.19 = (bf16[256,768]{1,0:T(8,128)(2,1)S(1)}, bf16[256,768]{1,0:T(8,128)(2,1)}, u32[]{:S(2)}) copy-start(bf16[256,768]{1,0:T(8,128)(2,1)} %param.11) | copy-start | bytes 1179652
  0.7 5.4 %copy-start.17 = (bf16[784,768]{1,0:T(8,128)(2,1)S(1)}, bf16[784,768]{1,0:T(8,128)(2,1)}, u32[]{:S(2)}) copy-start(bf16[784,768]{1,0:T(8,128)(2,1)} %video_ref.1) | copy-start | bytes 3612676
  6.1 1.3 copy-start.1
  6.1 1.6 copy-start.3
  6.1 2.0 copy-start.4
  8.1 26.3 %copy-start.2 = (bf16[784,768]{1,0:T(8,128)(2,1)}, bf16[784,768]{1,0:T(8,128)(2,1)S(1)}, u32[]{:S(2)}) copy-start(bf16[784,768]{1,0:T(8,128)(2,1)S(1)} %fusion.3.normed_ref) | copy-start | bytes 3612676
  34.5 1.0 copy-start.10
  35.5 1.0 copy-start.12
  36.5 3.1 %copy-start.8 = (bf16[5,256,768]{2,1,0:T(8,128)(2,1)}, bf16[5,256,768]{2,1,0:T(8,128)(2,1)S(1)}, u32[]{:S(2)}) copy-start(bf16[5,256,768]{2,1,0:T(8,128)(2,1)S(1)} %get-tuple-element.22) | copy-start | bytes 5898244
  38.0 1.7 copy-start.22
  39.7 1.7 copy-start.11
  39.7 1.7 copy-start.13
  39.7 1.7 copy-start.14
  80.7 1.0 copy-start.6
  81.8 1.0 copy-start.7
  82.8 1.3 copy-start.15
  93.0 4.6 %copy-start.9 = (bf16[5,256,768]{2,1,0:T(8,128)(2,1)S(1)}, bf16[5,256,768]{2,1,0:T(8,128)(2,1)}, u32[]{:S(2)}) copy-start(bf16[5,256,768]{2,1,0:T(8,128)(2,1)} %copy-done.8) | copy-start | bytes 5898244
  93.0 4.6 %copy-start.16 = (bf16[768,1280]{1,0:T(8,128)(2,1)S(1)}, bf16[768,1280]{1,0:T(8,128)(2,1)}, u32[]{:S(2)}) copy-start(bf16[768,1280]{1,0:T(8,128)(2,1)} %copy-done.15) | copy-start | bytes 5898244
  100.8 3.2 %copy-start.23 = (bf16[768,768]{1,0:T(8,128)(2,1)S(1)}, bf16[768,768]{1,0:T(8,128)(2,1)}, u32[]{:S(2)}) copy-start(bf16[768,768]{1,0:T(8,128)(2,1)} %param.13) | copy-start | bytes 3538948
  107.7 1.7 copy-start.5
  225.6 3.3 %copy-start.18 = (bf16[3,1024,768]{2,1,0:T(8,128)(2,1)S(1)}, bf16[3,1024,768]{2,1,0:T(8,128)(2,1)}, u32[]{:S(2)}) copy-start(bf16[3,1024,768]{2,1,0:T(8,128)(2,1)} %get-tuple-element.30) | copy-start | bytes 14155780
  228.9 3.9 %copy-start.21 = (bf16[784,768]{1,0:T(8,128)(2,1)S(1)}, bf16[784,768]{1,0:T(8,128)(2,1)}, u32[]{:S(2)}) copy-start(bf16[784,768]{1,0:T(8,128)(2,1)} %get-tuple-element.50) | copy-start | bytes 3612676
  232.8 1.7 copy-start.20
